TPU v7x, 512 devices: a whole 4x8x8 slice. The times are simulated.
512 devices in a mesh: tm: 16 (over x_hi, z), seq: 32 (over x_lo, y, core).
Axes of the slice: x: 4 (x_hi: 2, x_lo: 2; x = x_hi * 2 + x_lo), y: 8, z: 8, core: 2. Of those that a mesh axis runs over, the one named last changes fastest.
Arguments:
- queries: bfloat16 [16, 2048, 4096], P('tm', 'seq'), may hold values from -80 to 80, as said below
- keys: bfloat16 [16, 2048, 4096], P('tm', 'seq'), may hold values from -5 to 5
- values: bfloat16 [16, 2048, 4096], P('tm', 'seq'), may hold values from -6 to 6
- text_kv: bfloat16 [2, 2, 512, 4096], P(None, None, None, 'seq'), may hold values from -6 to 6
- trajectory: bfloat16 [16, 2048, 4096], P('tm', 'seq'), may hold values from -6 to 6
- start_latent: bfloat16 [2048, 4096], P('seq'), may hold values from -6 to 6
- region_mask: int32 [64], replicated, may hold values from 0 to 1
- timesteps: int32 [16, 2], P('tm'), may hold values from 123 to 999
Outputs:
- updated: float32 [16, 2048, 4096], P('tm', 'seq')
Inputs may be any that keep to these rules, and one draw needn't show every extreme that they name: `queries`: of order one and independent of the keys in the shown draw.
All inputs are finite; a program needn't handle non-finite values.
Results may differ from a plain program's by a relative error of at most 0.0009.
Values may be sent and summed in bfloat16 or wider, within the bound.
A program may use at most 64 MiB of HBM per device.

v0:
```python
import jax
import jax.numpy as jnp
from jax import lax
from jax.sharding import PartitionSpec as P

HD = 128
BLOCK = 32


def prefix(value, axis, join, neutral):
    count, mine = (lax.axis_size(axis), lax.axis_index(axis))
    pieces = lax.all_gather(value, axis)
    subtotal = jnp.full_like(value, 0) + jnp.asarray(neutral, value.dtype)

    def turn(position, subtotal):
        longer = join(subtotal, pieces[position])
        return jnp.where(position < mine, longer, subtotal)

    return lax.fori_loop(0, count - 1, turn, subtotal)


def attend(query_all, key_all, value_all, text_keys, text_values, heads_here, head_size):
    tokens = query_all.shape[0]
    row_count = min(512, tokens)
    block_count = tokens // row_count
    query_blocks = query_all.reshape(block_count, row_count, heads_here, head_size)
    key_heads = key_all.reshape(tokens, heads_here, head_size)
    value_heads = value_all.reshape(tokens, heads_here, head_size)
    text_key_heads = text_keys.reshape(2, -1, heads_here, head_size)
    text_value_heads = text_values.reshape(2, -1, heads_here, head_size)
    score_scale = head_size ** (-0.5)

    def one_block(query_block):
        video_score = (
            jnp.einsum("rhd,khd->hrk", query_block, key_heads, preferred_element_type=jnp.float32)
            * score_scale
        )
        text_score = (
            jnp.einsum(
                "rhd,bthd->bhrt", query_block, text_key_heads, preferred_element_type=jnp.float32
            )
            * score_scale
        )
        row_top = jnp.maximum(jnp.max(video_score, axis=-1)[None], jnp.max(text_score, axis=-1))
        video_prob = jnp.exp(video_score[None] - row_top[..., None])
        text_prob = jnp.exp(text_score - row_top[..., None])
        summed = jnp.sum(video_prob, axis=-1) + jnp.sum(text_prob, axis=-1)
        video_weight = (video_prob / summed[..., None]).astype(jnp.bfloat16)
        text_weight = (text_prob / summed[..., None]).astype(jnp.bfloat16)
        result = jnp.einsum(
            "bhrk,khd->brhd", video_weight, value_heads, preferred_element_type=jnp.float32
        )
        result = result + jnp.einsum(
            "bhrt,bthd->brhd", text_weight, text_value_heads, preferred_element_type=jnp.float32
        )
        return result.astype(jnp.bfloat16)

    results = lax.map(one_block, query_blocks)
    return results.transpose(1, 0, 2, 3, 4).reshape(2, tokens, heads_here * head_size)


def guide_mix(cond_branch, uncond_branch, token_mask, noise_level):
    cond_part = cond_branch.astype(jnp.float32)
    uncond_part = uncond_branch.astype(jnp.float32)
    strength = 1.0 + 5.0 * noise_level
    blended = jnp.where(
        token_mask[:, None] > 0, uncond_part + strength * (cond_part - uncond_part), cond_part
    )
    return blended.astype(jnp.bfloat16)


def add_terms(earlier, later):
    return earlier + later


def per_device(queries, keys, values, text_kv, trajectory, start_latent, region_mask, timesteps):
    head_size = HD
    tok_dev = queries.shape[1]
    query_all, key_all, value_all = (
        lax.all_to_all(queries[0], "seq", split_axis=1, concat_axis=0, tiled=True),
        lax.all_to_all(keys[0], "seq", split_axis=1, concat_axis=0, tiled=True),
        lax.all_to_all(values[0], "seq", split_axis=1, concat_axis=0, tiled=True),
    )
    heads_here = query_all.shape[1] // head_size
    branches = attend(
        query_all, key_all, value_all, text_kv[:, 0], text_kv[:, 1], heads_here, head_size
    )
    noise_level = timesteps[0, 0].astype(jnp.float32) / 1000.0
    step_length = (timesteps[0, 1] - timesteps[0, 0]).astype(jnp.float32) / 1000.0
    token_mask = jnp.repeat(region_mask, BLOCK)
    returned = lax.all_to_all(branches, "seq", split_axis=1, concat_axis=2, tiled=True)
    first_row = lax.axis_index("seq") * tok_dev
    own_mask = lax.dynamic_slice_in_dim(token_mask, first_row, tok_dev, 0)
    guided = guide_mix(returned[0], returned[1], own_mask, noise_level)
    drift = step_length * (
        (trajectory[0].astype(jnp.float32) - guided.astype(jnp.float32)) / noise_level
    )
    earlier_sum = prefix(drift, "tm", add_terms, jnp.zeros_like(drift))
    running = earlier_sum + drift
    return (start_latent.astype(jnp.float32) + running)[None]


def solution(mesh):
    return jax.shard_map(
        per_device,
        mesh=mesh,
        in_specs=(
            P("tm", "seq", None),
            P("tm", "seq", None),
            P("tm", "seq", None),
            P(None, None, None, "seq"),
            P("tm", "seq", None),
            P("seq", None),
            P(),
            P("tm", None),
        ),
        out_specs=P("tm", "seq", None),
        check_vma=False,
    )
```

profile of v0, /device:TPU:6, one launch (start us, length us, event | category | flops | bytes accessed | tf_op | source)
XLA Modules:
  0.0 415.9 jit_solution(17441901474533868384)
XLA Ops:
  8.8 8.7 %all-to-all-start = ((bf16[64,32,128]{2,0,1:T(8,128)(2,1)}), bf16[64,32,128]{2,0,1:T(8,128)(2,1)S(1)}, u32[]{:S(2)}, u32[]{:S(2)}) async-start(bf16[64,32,128]{2,0,1:T(8,128)(2,1)} %copy.69), calls=%async_computation | async-start | bytes 1048576 | tf_op jit(solution)/shard_map/all_to_all | solution.py:80
  19.6 15.0 %all-to-all-done = bf16[64,32,128]{2,0,1:T(8,128)(2,1)S(1)} async-done(((bf16[64,32,128]{2,0,1:T(8,128)(2,1)}), bf16[64,32,128]{2,0,1:T(8,128)(2,1)S(1)}, u32[]{:S(2)}, u32[]{:S(2)}) %all-to-all-start) | async-done | bytes 524320 | tf_op jit(solution)/shard_map/all_to_all | solution.py:80
  34.7 5.1 %all-to-all-start.1 = ((bf16[64,32,128]{2,0,1:T(8,128)(2,1)}), bf16[64,32,128]{2,0,1:T(8,128)(2,1)S(1)}, u32[]{:S(2)}, u32[]{:S(2)}) async-start(bf16[64,32,128]{2,0,1:T(8,128)(2,1)} %copy.70), calls=%async_computation.1 | async-start | bytes 1048576 | tf_op jit(solution)/shard_map/all_to_all | solution.py:81
  40.9 16.0 %all-to-all-done.1 = bf16[64,32,128]{2,0,1:T(8,128)(2,1)S(1)} async-done(((bf16[64,32,128]{2,0,1:T(8,128)(2,1)}), bf16[64,32,128]{2,0,1:T(8,128)(2,1)S(1)}, u32[]{:S(2)}, u32[]{:S(2)}) %all-to-all-start.1) | async-done | bytes 524320 | tf_op jit(solution)/shard_map/all_to_all | solution.py:81
  56.9 5.3 %all-to-all-start.2 = ((bf16[64,32,128]{2,0,1:T(8,128)(2,1)}), bf16[64,32,128]{2,0,1:T(8,128)(2,1)S(1)}, u32[]{:S(2)}, u32[]{:S(2)}) async-start(bf16[64,32,128]{2,0,1:T(8,128)(2,1)} %copy.72), calls=%async_computation.2 | async-start | bytes 1048576 | tf_op jit(solution)/shard_map/all_to_all | solution.py:82
  62.9 16.3 %all-to-all-done.2 = bf16[64,32,128]{2,0,1:T(8,128)(2,1)S(1)} async-done(((bf16[64,32,128]{2,0,1:T(8,128)(2,1)}), bf16[64,32,128]{2,0,1:T(8,128)(2,1)S(1)}, u32[]{:S(2)}, u32[]{:S(2)}) %all-to-all-start.2) | async-done | bytes 524320 | tf_op jit(solution)/shard_map/all_to_all | solution.py:82
  79.3 23.2 %while.24 = (s32[]{:T(128)}, bf16[4,2,512,1,128]{4,2,0,1,3:T(8,128)(2,1)S(1)}, bf16[4,512,1,128]{3,1,2,0:T(8,128)(2,1)S(1)}, bf16[2048,1,128]{2,0,1:T(8,128)(2,1...) while((s32[]{:T(128)}, ...), condition=%wide.region_5.6_spmd, body=%wide.region_0.5_spmd.sunk | while | flops 1091303936 | bytes 23130236 | solution.py:58
  83.0 2.0 fusion.46
  88.8 2.0 fusion.46
  94.6 2.0 fusion.46
  100.5 2.0 fusion.46
  102.5 9.5 %copy.75 = bf16[2,2048,128]{2,0,1:T(2,128)(2,1)} copy(bf16[2,2048,128]{2,1,0:T(8,128)(2,1)S(1)} %bitcast.187) | data formatting | bytes 2097152 | tf_op jit(solution)/shard_map/reshape | solution.py:59
  112.0 5.3 %all-to-all-start.3 = ((bf16[2,2048,128]{2,0,1:T(2,128)(2,1)}), bf16[2,2048,128]{2,0,1:T(2,128)(2,1)S(1)}, u32[]{:S(2)}, u32[]{:S(2)}) async-start(bf16[2,2048,128]{2,0,1:T(2,128)(2,1)} %copy.75), calls=%async_computation.3 | async-start | bytes 2097152 | tf_op jit(solution)/shard_map/all_to_all | solution.py:91
  120.2 24.4 %all-to-all-done.3 = bf16[2,2048,128]{2,0,1:T(2,128)(2,1)S(1)} async-done(((bf16[2,2048,128]{2,0,1:T(2,128)(2,1)}), bf16[2,2048,128]{2,0,1:T(2,128)(2,1)S(1)}, u32[]{:S(2)}, u32[]{:S(2)}) %all-to-all-start.3) | async-done | bytes 1048608 | tf_op jit(solution)/shard_map/all_to_all | solution.py:91
  146.2 2.8 fusion.23
  151.2 229.5 %all-gather.2.cloned.1.call-done = f32[16,64,4096]{2,1,0:T(8,128)} async-done(((f32[1,64,4096]{2,1,0:T(8,128)}), f32[16,64,4096]{2,1,0:T(8,128)}) %all-gather.2.cloned.1.call-update) | async-done | bytes 16777232 | tf_op jit(solution)/shard_map/all_gather | solution.py:12
  380.7 24.2 %while.25 = (s32[]{:T(128)}, f32[64,4096]{1,0:T(8,128)S(1)}, s32[]{:T(128)}, f32[16,64,4096]{2,1,0:T(8,128)}, s32[]{:T(128)}, /*index=5*/s32[]{:T(128)}) while((s32[]{:T(128)}, f32[64,4096]{1,0:T(8,128)S(1)}, s32[]{:T(128)}, f32[16,64,4096]{2,1,0:T(8,128)}, s32[]{:T(128)}, /*index=5*/s32[]{:T(128)}) %tuple.58), condition=%wide.region_7.8_spmd.clone, body=%wide.region_6.7_spmd.clone.sunk | while | flops 786436 | bytes 3145821 | solution.py:19
  380.7 1.7 add_select_fusion.2
  382.4 1.6 add_select_fusion.2
  384.0 1.6 add_select_fusion.2
  385.6 1.6 add_select_fusion.2
  387.2 1.6 add_select_fusion.2
  398.5 1.6 add_select_fusion.2
  405.0 4.1 fusion.29
  (78 shorter events, 40.2 us)
Async XLA Ops:
  6.5 33.3 %copy-start.2 = (bf16[1,64,4096]{2,1,0:T(8,128)(2,1)S(1)}, bf16[1,64,4096]{2,1,0:T(8,128)(2,1)}, u32[]{:S(2)}) copy-start(bf16[1,64,4096]{2,1,0:T(8,128)(2,1)} %param.14) | copy-start | bytes 1572868
  7.7 54.4 %copy-start.3 = (bf16[2,2,512,128]{3,2,1,0:T(8,128)(2,1)S(1)}, bf16[2,2,512,128]{3,2,1,0:T(8,128)(2,1)}, u32[]{:S(2)}) copy-start(bf16[2,2,512,128]{3,2,1,0:T(8,128)(2,1)} %param.15) | copy-start | bytes 1572868
  8.8 25.9 %all-to-all-start = ((bf16[64,32,128]{2,0,1:T(8,128)(2,1)}), bf16[64,32,128]{2,0,1:T(8,128)(2,1)S(1)}, u32[]{:S(2)}, u32[]{:S(2)}) async-start(bf16[64,32,128]{2,0,1:T(8,128)(2,1)} %copy.69), calls=%async_computation | async-start | bytes 1048576 | tf_op jit(solution)/shard_map/all_to_all | solution.py:80
  34.7 22.2 %all-to-all-start.1 = ((bf16[64,32,128]{2,0,1:T(8,128)(2,1)}), bf16[64,32,128]{2,0,1:T(8,128)(2,1)S(1)}, u32[]{:S(2)}, u32[]{:S(2)}) async-start(bf16[64,32,128]{2,0,1:T(8,128)(2,1)} %copy.70), calls=%async_computation.1 | async-start | bytes 1048576 | tf_op jit(solution)/shard_map/all_to_all | solution.py:81
  56.9 22.4 %all-to-all-start.2 = ((bf16[64,32,128]{2,0,1:T(8,128)(2,1)}), bf16[64,32,128]{2,0,1:T(8,128)(2,1)S(1)}, u32[]{:S(2)}, u32[]{:S(2)}) async-start(bf16[64,32,128]{2,0,1:T(8,128)(2,1)} %copy.72), calls=%async_computation.2 | async-start | bytes 1048576 | tf_op jit(solution)/shard_map/all_to_all | solution.py:82
  80.0 2.3 copy-start.4
  85.9 2.3 copy-start.4
  91.7 2.3 copy-start.4
  97.5 2.3 copy-start.4
  102.5 15.0 %copy-start.6 = (s32[64]{0:T(128)S(1)}, s32[64]{0:T(128)}, u32[]{:S(2)}) copy-start(s32[64]{0:T(128)} %param.18) | copy-start | bytes 772
  102.5 15.2 %copy-start.5 = (s32[1,2]{1,0:T(1,128)S(1)}, s32[1,2]{1,0:T(1,128)}, u32[]{:S(2)}) copy-start(s32[1,2]{1,0:T(1,128)} %param.19) | copy-start | bytes 28
  112.0 32.6 %all-to-all-start.3 = ((bf16[2,2048,128]{2,0,1:T(2,128)(2,1)}), bf16[2,2048,128]{2,0,1:T(2,128)(2,1)S(1)}, u32[]{:S(2)}, u32[]{:S(2)}) async-start(bf16[2,2048,128]{2,0,1:T(2,128)(2,1)} %copy.75), calls=%async_computation.3 | async-start | bytes 2097152 | tf_op jit(solution)/shard_map/all_to_all | solution.py:91
  117.3 263.4 %all-gather.2.cloned.1.call-start = ((), (), s32[]{:S(2)}) async-start(), calls=%async_computation.4 | async-start | bytes 17825792 | tf_op jit(solution)/shard_map/all_gather | solution.py:12
  144.7 1.5 copy-start.1
  380.7 24.2 %copy-start = (f32[1,64,32,128]{3,2,1,0:T(8,128)S(1)}, f32[1,64,32,128]{3,2,1,0:T(8,128)}, u32[]{:S(2)}) copy-start(f32[1,64,32,128]{3,2,1,0:T(8,128)} %copy.83) | copy-start | bytes 3145732
Sparse Core Ops, SparseCore 0:
  149.2 231.5 all-gather.1
where the time goes:
time: 419 us; the launch traced here: 416 us
  waiting for transfers between devices  301 us (72%)
  other arithmetic  38.3 us (9%)
  starting transfers between devices  24.6 us (6%)
  local copies, waits for them, and re-layouts  20 us (5%)
  matrix products  15.7 us (4%)
  between operations  15.4 us (4%)
    all_gather x1, waiting for transfers between devices, prefix(): pieces = lax.all_gather(value, axis)  229 us
    all_to_all x1, waiting for transfers between devices, per_device(): lax.all_to_all(branches, 'seq', split_axis=1, concat_axis=2, tiled=True)  24.4 us
    select_n x15, other arithmetic, turn(): return jnp.where(position < mine, longer, subtotal)  23.9 us
    all_to_all x1, waiting for transfers between devices, per_device(): lax.all_to_all(values[0], 'seq', split_axis=1, concat_axis=0, tiled=True)  16.3 us
    all_to_all x1, waiting for transfers between devices, per_device(): lax.all_to_all(keys[0], 'seq', split_axis=1, concat_axis=0, tiled=True)  16 us
    all_to_all x1, waiting for transfers between devices, per_device(): lax.all_to_all(queries[0], 'seq', split_axis=1, concat_axis=0, tiled=True)  15 us
    reshape x1, local copies, waits for them, and re-layouts, attend(): results.transpose(1, 0, 2, 3, 4).reshape(2, tokens, heads_here * head_size)  9.46 us
    all_to_all x1, starting transfers between devices, per_device(): lax.all_to_all(queries[0], 'seq', split_axis=1, concat_axis=0, tiled=True)  8.72 us
  transfers between devices with their start and end apart: 5, of which 5 were waited for; matrix products, arithmetic and copies ran while one was open for 2% of the time, Pallas kernels for 0%

commit v1 on v0

v1 whole, which is shorter than its diff:
```python
import jax
import jax.numpy as jnp
from jax import lax
from jax.experimental import pallas as pl
from jax.experimental.pallas import tpu as pltpu
from jax.sharding import PartitionSpec as P

HD = 128
BLOCK = 32
TOK = 64
HALF = 32
NT = 32
NZ = 8
ROUNDS = 8
LAG1 = 1
LAG2 = 2
MESH = pl.DeviceIdType.MESH
F32 = jnp.float32
BF16 = jnp.bfloat16


def y_offset(r):
    half = (r + 1) // 2
    return jnp.where(r % 2 == 1, half, (8 - half) % 8)


def take_all(ref, sem):
    pltpu.make_async_copy(ref, ref, sem).wait()


def kernel(
    mask_ref, ts_ref, q_ref, k_ref, v_ref, text_ref, traj_ref, start_ref, out_ref,
    kbuf, vbuf, qbuf, text, gbuf, rbuf, pbuf, tjbuf, stbuf, totbuf, base, obuf, coef,
    k_sem, v_sem, q_sem, r_sem, p_sem, tj_sem, st_sem, tot_sem, o_sem, c_sem, text_sem,
    ks_sem, vs_sem, qs_sem, rs_sem, ps_sem, tjs_sem, tots_sem, os_sem, cs_sem,
):
    tm, seq = lax.axis_index("tm"), lax.axis_index("seq")
    xh, z = tm // NZ, tm % NZ
    x, y, c = seq // 16, (seq // 2) % 8, seq % 2
    mine = x * 2 + c

    def seq_peer(n):
        yy = (y + y_offset(n // 4)) % 8
        return ((x + (n // 2) % 2) % 2) * 16 + yy * 2 + (c + n % 2) % 2

    def columns(head):
        return pl.ds(pl.multiple_of(head * HD, HD), HD)

    def rows(index, size):
        return pl.ds(pl.multiple_of(index * size, size), size)

    barrier = pltpu.get_barrier_semaphore()

    def greet_seq(n, carry):
        pl.semaphore_signal(barrier, inc=1, device_id=(tm, seq_peer(n)), device_id_type=MESH)
        return carry

    def greet_z(n, carry):
        pl.semaphore_signal(
            barrier, inc=1, device_id=(xh * NZ + (z + n) % NZ, seq), device_id_type=MESH
        )
        return carry

    lax.fori_loop(1, NT, greet_seq, 0)
    lax.fori_loop(1, NZ, greet_z, 0)
    pl.semaphore_signal(barrier, inc=1, device_id=((1 - xh) * NZ + z, seq), device_id_type=MESH)

    role_a, role_h = z // 2, z % 2
    pltpu.make_async_copy(text_ref, text, text_sem).start()
    pltpu.make_async_copy(k_ref.at[:, columns(seq)], kbuf.at[rows(seq, TOK)], k_sem).start()
    pltpu.make_async_copy(v_ref.at[:, columns(seq)], vbuf.at[rows(seq, TOK)], v_sem).start()
    pltpu.make_async_copy(q_ref.at[:, columns(seq)], qbuf.at[0, mine], q_sem.at[0]).start()

    def head_of(a, r):
        return (a // 2) * 16 + ((y + y_offset(r)) % 8) * 2 + a % 2

    def local_tiles(r, carry):
        window = (rows(role_h, HALF), columns(head_of(role_a, r)))
        pltpu.make_async_copy(start_ref.at[window], stbuf.at[r], st_sem).start()
        pltpu.make_async_copy(traj_ref.at[window], tjbuf.at[r, z], tj_sem).start()
        return carry

    lax.fori_loop(0, ROUNDS, local_tiles, 0)

    now = jnp.full((8, HD), ts_ref[0, 0], jnp.int32).astype(F32)
    length = jnp.full((8, HD), ts_ref[0, 1] - ts_ref[0, 0], jnp.int32).astype(F32) / 1000.0
    noise = now / 1000.0
    strength = (1.0 + 5.0 * noise)[:1]
    coef[z] = length / noise

    pl.semaphore_wait(barrier, NT - 1 + NZ - 1 + 1)

    def send_k(n, carry):
        peer = seq_peer(n)
        pltpu.make_async_remote_copy(
            k_ref.at[:, columns(peer)], kbuf.at[rows(seq, TOK)], ks_sem, k_sem,
            device_id=(tm, peer), device_id_type=MESH,
        ).start()
        return carry

    def send_v(n, carry):
        peer = seq_peer(n)
        pltpu.make_async_remote_copy(
            v_ref.at[:, columns(peer)], vbuf.at[rows(seq, TOK)], vs_sem, v_sem,
            device_id=(tm, peer), device_id_type=MESH,
        ).start()
        return carry

    def send_q(n, carry):
        peer = seq_peer(n)
        pltpu.make_async_remote_copy(
            q_ref.at[:, columns(peer)], qbuf.at[n // 4, mine], qs_sem, q_sem.at[n // 4],
            device_id=(tm, peer), device_id_type=MESH,
        ).start()
        return carry

    def send_coef(n, carry):
        pltpu.make_async_remote_copy(
            coef.at[z], coef.at[z], cs_sem, c_sem,
            device_id=(xh * NZ + (z + n) % NZ, seq), device_id_type=MESH,
        ).start()
        return carry

    def send_traj(n, carry):
        other = (z + 1 + n // ROUNDS) % NZ
        r = n % ROUNDS
        window = (rows(other % 2, HALF), columns(head_of(other // 2, r)))
        pltpu.make_async_remote_copy(
            traj_ref.at[window], tjbuf.at[r, z], tjs_sem, tj_sem,
            device_id=(xh * NZ + other, seq), device_id_type=MESH,
        ).start()
        return carry

    lax.fori_loop(1, NT, send_k, 0)
    lax.fori_loop(1, NT, send_v, 0)
    lax.fori_loop(1, NZ, send_coef, 0)
    lax.fori_loop(1, NT, send_q, 0)
    lax.fori_loop(0, (NZ - 1) * ROUNDS, send_traj, 0)

    take_all(text_ref, text_sem)
    take_all(kbuf, k_sem)
    take_all(vbuf, v_sem)

    scale = HD ** (-0.5)
    nt = (((1,), (1,)), ((), ()))

    def attention(r):
        take_all(qbuf.at[r], q_sem.at[r])
        q = qbuf[r].reshape(4 * TOK, HD)
        sv = lax.dot_general(q, kbuf[...], nt, preferred_element_type=F32) * scale
        mv = jnp.max(sv, axis=-1, keepdims=True)
        pv = jnp.exp(sv - mv)
        lv = jnp.sum(pv, axis=-1, keepdims=True)
        branch = []
        for b in range(2):
            st = lax.dot_general(q, text[b, 0], nt, preferred_element_type=F32) * scale
            top = jnp.maximum(mv, jnp.max(st, axis=-1, keepdims=True))
            pt = jnp.exp(st - top)
            shift = jnp.exp(mv - top)
            inverse = 1.0 / (lv * shift + jnp.sum(pt, axis=-1, keepdims=True))
            wv = (pv * (shift * inverse)).astype(BF16)
            wt = (pt * inverse).astype(BF16)
            o = jnp.dot(wv, vbuf[...], preferred_element_type=F32)
            o = o + jnp.dot(wt, text[b, 1], preferred_element_type=F32)
            branch.append(o.astype(BF16).astype(F32))
        cond, uncond = branch
        mixed = uncond + strength * (cond - uncond)
        ys = (y + 8 - y_offset(r)) % 8
        for j in range(4):
            token_block = ((j // 2) * 16 + ys * 2 + j % 2) * 2
            for h in range(2):
                part = slice((2 * j + h) * BLOCK, (2 * j + h + 1) * BLOCK)
                guided_here = jnp.full((BLOCK, HD), mask_ref[token_block + h], jnp.int32) > 0
                gbuf[r, j, h * BLOCK : (h + 1) * BLOCK] = jnp.where(
                    guided_here, mixed[part], cond[part]
                ).astype(BF16)

        def send_back(j, carry):
            peer = (j // 2) * 16 + ys * 2 + j % 2

            @pl.when(peer == seq)
            def _():
                pltpu.make_async_copy(gbuf.at[r, j], rbuf.at[r, mine], r_sem.at[r]).start()

            @pl.when(peer != seq)
            def _():
                pltpu.make_async_remote_copy(
                    gbuf.at[r, j], rbuf.at[r, mine], rs_sem, r_sem.at[r],
                    device_id=(tm, peer), device_id_type=MESH,
                ).start()

            return carry

        lax.fori_loop(0, 4, send_back, 0)

    def to_steps(r):
        take_all(rbuf.at[r], r_sem.at[r])
        pltpu.make_async_copy(
            rbuf.at[r, role_a, rows(role_h, HALF)], pbuf.at[r, z], p_sem.at[r]
        ).start()

        def send(n, carry):
            other = (z + n) % NZ
            pltpu.make_async_remote_copy(
                rbuf.at[r, other // 2, rows(other % 2, HALF)], pbuf.at[r, z], ps_sem, p_sem.at[r],
                device_id=(xh * NZ + other, seq), device_id_type=MESH,
            ).start()
            return carry

        lax.fori_loop(1, NZ, send, 0)

    def running_sum(r):
        take_all(pbuf.at[r], p_sem.at[r])

        @pl.when(xh == 0)
        def _():
            base[...] = stbuf[r].astype(F32)

        @pl.when(xh == 1)
        def _():
            take_all(totbuf.at[r], tot_sem.at[r])
            base[...] = totbuf[r]

        total = base[...]
        for k in range(NZ):
            drift = coef[k, 0:1] * (tjbuf[r, k].astype(F32) - pbuf[r, k].astype(F32))
            total = total + drift
            obuf[r, k] = total

        @pl.when(xh == 0)
        def _():
            pltpu.make_async_remote_copy(
                obuf.at[r, NZ - 1], totbuf.at[r], tots_sem, tot_sem.at[r],
                device_id=(NZ + z, seq), device_id_type=MESH,
            ).start()

        window = (rows(role_h, HALF), columns(head_of(role_a, r)))
        pltpu.make_async_copy(obuf.at[r, z], out_ref.at[window], o_sem).start()

        def send(n, carry):
            other = (z + n) % NZ
            pltpu.make_async_remote_copy(
                obuf.at[r, other], out_ref.at[window], os_sem, o_sem,
                device_id=(xh * NZ + other, seq), device_id_type=MESH,
            ).start()
            return carry

        lax.fori_loop(1, NZ, send, 0)

    def turn(t, carry):
        @pl.when(t < ROUNDS)
        def _():
            attention(t)

        @pl.when((t >= LAG1) & (t < ROUNDS + LAG1))
        def _():
            to_steps(t - LAG1)

        @pl.when(t == LAG2)
        def _():
            take_all(stbuf, st_sem)
            take_all(tjbuf, tj_sem)
            take_all(coef.at[0 : NZ - 1], c_sem)

        @pl.when(t >= LAG2)
        def _():
            running_sum(t - LAG2)

        return carry

    lax.fori_loop(0, ROUNDS + LAG2, turn, 0)

    take_all(kbuf.at[0 : (NT - 1) * TOK], ks_sem)
    take_all(vbuf.at[0 : (NT - 1) * TOK], vs_sem)
    take_all(kbuf.at[0 : (NT - 1) * TOK], qs_sem)
    take_all(kbuf.at[0 : (NT - 1) * TOK], rs_sem)
    take_all(tjbuf.at[:, 0 : NZ - 1], tjs_sem)
    take_all(pbuf.at[:, 0 : NZ - 1], ps_sem)
    take_all(obuf.at[:, 0 : NZ - 1], os_sem)
    take_all(coef.at[0 : NZ - 1], cs_sem)

    @pl.when(xh == 0)
    def _():
        take_all(totbuf, tots_sem)

    take_all(out_ref, o_sem)


def per_device(queries, keys, values, text_kv, trajectory, start_latent, region_mask, timesteps):
    any_space = pl.BlockSpec(memory_space=pl.ANY)
    smem = pl.BlockSpec(memory_space=pltpu.SMEM)
    dma, dma8 = pltpu.SemaphoreType.DMA, pltpu.SemaphoreType.DMA((ROUNDS,))
    out = pl.pallas_call(
        kernel,
        out_shape=jax.ShapeDtypeStruct(queries.shape[1:], F32),
        in_specs=[smem, smem] + [any_space] * 6,
        out_specs=any_space,
        scratch_shapes=[
            pltpu.VMEM((NT * TOK, HD), BF16),
            pltpu.VMEM((NT * TOK, HD), BF16),
            pltpu.VMEM((ROUNDS, 4, TOK, HD), BF16),
            pltpu.VMEM(text_kv.shape, BF16),
            pltpu.VMEM((ROUNDS, 4, TOK, HD), BF16),
            pltpu.VMEM((ROUNDS, 4, TOK, HD), BF16),
            pltpu.VMEM((ROUNDS, NZ, HALF, HD), BF16),
            pltpu.VMEM((ROUNDS, NZ, HALF, HD), BF16),
            pltpu.VMEM((ROUNDS, HALF, HD), BF16),
            pltpu.VMEM((ROUNDS, HALF, HD), F32),
            pltpu.VMEM((HALF, HD), F32),
            pltpu.VMEM((ROUNDS, NZ, HALF, HD), F32),
            pltpu.VMEM((NZ, 8, HD), F32),
            dma, dma, dma8, dma8, dma8, dma, dma, dma8, dma, dma, dma,
            dma, dma, dma, dma, dma, dma, dma, dma, dma,
        ],
        compiler_params=pltpu.CompilerParams(
            collective_id=0, has_side_effects=True, vmem_limit_bytes=48 << 20
        ),
    )(
        region_mask, timesteps, queries[0], keys[0], values[0], text_kv, trajectory[0], start_latent
    )
    return out[None]


def solution(mesh):
    return jax.shard_map(
        per_device,
        mesh=mesh,
        in_specs=(
            P("tm", "seq", None),
            P("tm", "seq", None),
            P("tm", "seq", None),
            P(None, None, None, "seq"),
            P("tm", "seq", None),
            P("seq", None),
            P(),
            P("tm", None),
        ),
        out_specs=P("tm", "seq", None),
        check_vma=False,
    )
```

time: 419 us -> 104 us (0.25)
  waiting for transfers between devices: 301 us -> 0 us
  Pallas kernels: 0 us -> 95.5 us
  other arithmetic: 38.3 us -> 0 us
  starting transfers between devices: 24.6 us -> 0 us
  matrix products: 15.7 us -> 0 us
  between operations: 15.4 us -> 0.02 us
  local copies, waits for them, and re-layouts: 20 us -> 7.89 us
    all_gather x1 -> x0, waiting for transfers between devices: 229 us -> none  [prefix(): pieces = lax.all_gather(value, axis)]
    pallas_call x0 -> x1, Pallas kernels: none -> 95.5 us  [per_device(): pl.pallas_call(kernel, out_shape=jax.ShapeDtypeStruct(queries.shape[1:],...]
    all_to_all x4 -> x0, waiting for transfers between devices: 71.8 us -> none  [the longest x1 24.4 us: per_device(): lax.all_to_all(branches, 'seq', split_axis=1, concat_axis=2, tiled=True)]
    all_to_all x4 -> x0, starting transfers between devices: 24.4 us -> none  [the longest x1 8.72 us: per_device(): lax.all_to_all(queries[0], 'seq', split_axis=1, concat_axis=0, tiled=True)]
    select_n x15 -> x0, other arithmetic: 23.9 us -> none  [turn(): return jnp.where(position < mine, longer, subtotal)]
    dot_general x16 -> x0, matrix products: 15.7 us -> none  [the longest x4 8.06 us: one_block(): jnp.einsum('bhrk,khd->brhd', video_weight, value_heads, preferred_element...]
    reshape x2 -> x0, local copies, waits for them, and re-layouts: 9.53 us -> none  [the longest x1 9.46 us: attend(): results.transpose(1, 0, 2, 3, 4).reshape(2, tokens, heads_here * head_size)]
    reduce_sum x8 -> x0, other arithmetic: 7.17 us -> none  [one_block(): summed = jnp.sum(video_prob, axis=-1) + jnp.sum(text_prob, axis=-1)]
  transfers between devices with their start and end apart: 5 -> 0, of which waited for: 5 -> 0; matrix products, arithmetic and copies ran while one was open for 2% -> 0% of each run, Pallas kernels for 0% -> 0%
where the time goes in v1:
time: 104 us; the launch traced here: 103 us
  Pallas kernels  95.5 us (92%)
  local copies, waits for them, and re-layouts  7.89 us (8%)
    pallas_call x1, Pallas kernels, per_device(): pl.pallas_call(kernel, out_shape=jax.ShapeDtypeStruct(queries.shape[1:],...  95.5 us
    unnamed x17, local copies, waits for them, and re-layouts  7.89 us

profile of v1, /device:TPU:6, one launch (start us, length us, event | category | flops | bytes accessed | tf_op | source)
XLA Modules:
  0.0 103.4 jit_solution(1081295284782856964)
XLA Ops:
  0.0 0.0 copy-start.6
  0.0 0.0 copy-start.7
  0.0 0.7 copy-done.6
  0.7 0.0 copy-done.7
  0.7 0.0 copy-start
  0.7 1.0 %copy-done = bf16[1,64,4096]{2,1,0:T(8,128)(2,1)S(1)} copy-done((bf16[1,64,4096]{2,1,0:T(8,128)(2,1)S(1)}, bf16[1,64,4096]{2,1,0:T(8,128)(2,1)}, u32[]{:S(2)}) %copy-start) | copy-done | bytes 524312
  1.7 0.0 copy-start.1
  1.7 1.0 %copy-done.1 = bf16[1,64,4096]{2,1,0:T(8,128)(2,1)S(1)} copy-done((bf16[1,64,4096]{2,1,0:T(8,128)(2,1)S(1)}, bf16[1,64,4096]{2,1,0:T(8,128)(2,1)}, u32[]{:S(2)}) %copy-start.1) | copy-done | bytes 524312
  2.8 0.0 copy-start.2
  2.8 1.0 %copy-done.2 = bf16[1,64,4096]{2,1,0:T(8,128)(2,1)S(1)} copy-done((bf16[1,64,4096]{2,1,0:T(8,128)(2,1)S(1)}, bf16[1,64,4096]{2,1,0:T(8,128)(2,1)}, u32[]{:S(2)}) %copy-start.2) | copy-done | bytes 524312
  3.8 0.0 copy-start.3
  3.8 1.0 %copy-done.3 = bf16[2,2,512,128]{3,2,1,0:T(8,128)(2,1)S(1)} copy-done((bf16[2,2,512,128]{3,2,1,0:T(8,128)(2,1)S(1)}, bf16[2,2,512,128]{3,2,1,0:T(8,128)(2,1)}, u32[]{:S(2)}) %copy-start.3) | copy-done | bytes 524312
  4.8 0.0 copy-start.4
  4.8 1.0 %copy-done.4 = bf16[1,64,4096]{2,1,0:T(8,128)(2,1)S(1)} copy-done((bf16[1,64,4096]{2,1,0:T(8,128)(2,1)S(1)}, bf16[1,64,4096]{2,1,0:T(8,128)(2,1)}, u32[]{:S(2)}) %copy-start.4) | copy-done | bytes 524312
  5.9 0.0 copy-start.5
  5.9 1.0 %copy-done.5 = bf16[64,4096]{1,0:T(8,128)(2,1)S(1)} copy-done((bf16[64,4096]{1,0:T(8,128)(2,1)S(1)}, bf16[64,4096]{1,0:T(8,128)(2,1)}, u32[]{:S(2)}) %copy-start.5) | copy-done | bytes 524312
  6.9 95.5 %shard_map.82 = f32[64,4096]{1,0:T(8,128)S(1)} custom-call(s32[64]{0:T(128)S(1)} %copy-done.6, s32[1,2]{1,0:T(1,128)S(1)} %copy-done.7, bf16[64,4096]{1,0:T(8,128)(2,1)S(1)} %bitcast.6, bf16[64,4096]{1,0:T(8,128)(2,1)S(1)} %bitcast.7, bf16[64,4096]{1,0:T(8,128)(2,1)S(1)} %bitcast.8, bf16[2,2,512,128]{3,2,1,0:T(8,128)(2,1)S(1)} %copy-done.3, ...), custom_call_target="tpu_custom_call" | custom-call | tf_op jit(solution)/shard_map/pallas_call | solution.py:293
  102.5 1.0 copy.10
Async XLA Ops:
  0.0 0.7 copy-start.6
  0.0 0.7 copy-start.7
  0.7 1.0 %copy-start = (bf16[1,64,4096]{2,1,0:T(8,128)(2,1)S(1)}, bf16[1,64,4096]{2,1,0:T(8,128)(2,1)}, u32[]{:S(2)}) copy-start(bf16[1,64,4096]{2,1,0:T(8,128)(2,1)} %param.8) | copy-start | bytes 1572868
  1.7 1.0 %copy-start.1 = (bf16[1,64,4096]{2,1,0:T(8,128)(2,1)S(1)}, bf16[1,64,4096]{2,1,0:T(8,128)(2,1)}, u32[]{:S(2)}) copy-start(bf16[1,64,4096]{2,1,0:T(8,128)(2,1)} %param.9) | copy-start | bytes 1572868
  2.8 1.0 %copy-start.2 = (bf16[1,64,4096]{2,1,0:T(8,128)(2,1)S(1)}, bf16[1,64,4096]{2,1,0:T(8,128)(2,1)}, u32[]{:S(2)}) copy-start(bf16[1,64,4096]{2,1,0:T(8,128)(2,1)} %param.10) | copy-start | bytes 1572868
  3.8 1.0 %copy-start.3 = (bf16[2,2,512,128]{3,2,1,0:T(8,128)(2,1)S(1)}, bf16[2,2,512,128]{3,2,1,0:T(8,128)(2,1)}, u32[]{:S(2)}) copy-start(bf16[2,2,512,128]{3,2,1,0:T(8,128)(2,1)} %text_ref.1) | copy-start | bytes 1572868
  4.8 1.0 %copy-start.4 = (bf16[1,64,4096]{2,1,0:T(8,128)(2,1)S(1)}, bf16[1,64,4096]{2,1,0:T(8,128)(2,1)}, u32[]{:S(2)}) copy-start(bf16[1,64,4096]{2,1,0:T(8,128)(2,1)} %param.12) | copy-start | bytes 1572868
  5.9 1.0 %copy-start.5 = (bf16[64,4096]{1,0:T(8,128)(2,1)S(1)}, bf16[64,4096]{1,0:T(8,128)(2,1)}, u32[]{:S(2)}) copy-start(bf16[64,4096]{1,0:T(8,128)(2,1)} %start_ref.1) | copy-start | bytes 1572868

commit v2 on v1

--- a/solution.py
+++ b/solution.py
@@ -1,3 +1,5 @@
+import math
+
 import jax
 import jax.numpy as jnp
 from jax import lax
@@ -12,8 +14,8 @@
 NT = 32
 NZ = 8
 ROUNDS = 8
-LAG1 = 1
-LAG2 = 2
+LAGS = (0, 2, 4, 6, 8)
+BEHIND = 2
 MESH = pl.DeviceIdType.MESH
 F32 = jnp.float32
 BF16 = jnp.bfloat16
@@ -30,9 +32,11 @@
 
 def kernel(
     mask_ref, ts_ref, q_ref, k_ref, v_ref, text_ref, traj_ref, start_ref, out_ref,
-    kbuf, vbuf, qbuf, text, gbuf, rbuf, pbuf, tjbuf, stbuf, totbuf, base, obuf, coef,
-    k_sem, v_sem, q_sem, r_sem, p_sem, tj_sem, st_sem, tot_sem, o_sem, c_sem, text_sem,
-    ks_sem, vs_sem, qs_sem, rs_sem, ps_sem, tjs_sem, tots_sem, os_sem, cs_sem,
+    mask, ts, kbuf, vbuf, qbuf, text, own, gbuf, rbuf, pbuf, tjbuf, stbuf, totbuf, base, sums, last,
+    fin, obuf, coef,
+    small_sem, k_sem, v_sem, q_sem, r_sem, p_sem, tj_sem, st_sem, tot_sem, f_sem, l_sem, o_sem,
+    c_sem, text_sem, own_sem,
+    ks_sem, vs_sem, qs_sem, rs_sem, ps_sem, tjs_sem, tots_sem, fs_sem, ls_sem, cs_sem,
 ):
     tm, seq = lax.axis_index("tm"), lax.axis_index("seq")
     xh, z = tm // NZ, tm % NZ
@@ -66,6 +70,10 @@
     pl.semaphore_signal(barrier, inc=1, device_id=((1 - xh) * NZ + z, seq), device_id_type=MESH)
 
     role_a, role_h = z // 2, z % 2
+    partner = z + 1 - 2 * role_h
+    pltpu.make_async_copy(mask_ref, mask, small_sem.at[0]).start()
+    pltpu.make_async_copy(ts_ref, ts, small_sem.at[1]).start()
+    pltpu.make_async_copy(traj_ref, own, own_sem).start()
     pltpu.make_async_copy(text_ref, text, text_sem).start()
     pltpu.make_async_copy(k_ref.at[:, columns(seq)], kbuf.at[rows(seq, TOK)], k_sem).start()
     pltpu.make_async_copy(v_ref.at[:, columns(seq)], vbuf.at[rows(seq, TOK)], v_sem).start()
@@ -82,8 +90,11 @@
 
     lax.fori_loop(0, ROUNDS, local_tiles, 0)
 
-    now = jnp.full((8, HD), ts_ref[0, 0], jnp.int32).astype(F32)
-    length = jnp.full((8, HD), ts_ref[0, 1] - ts_ref[0, 0], jnp.int32).astype(F32) / 1000.0
+    pltpu.make_async_copy(mask_ref, mask, small_sem.at[0]).wait()
+    pltpu.make_async_copy(ts_ref, ts, small_sem.at[1]).wait()
+
+    now = jnp.full((8, HD), ts[0, 0], jnp.int32).astype(F32)
+    length = jnp.full((8, HD), ts[0, 1] - ts[0, 0], jnp.int32).astype(F32) / 1000.0
     noise = now / 1000.0
     strength = (1.0 + 5.0 * noise)[:1]
     coef[z] = length / noise
@@ -91,7 +102,7 @@
     pl.semaphore_wait(barrier, NT - 1 + NZ - 1 + 1)
 
     def send_k(n, carry):
-        peer = seq_peer(n)
+        peer = seq_peer(NT - n)
         pltpu.make_async_remote_copy(
             k_ref.at[:, columns(peer)], kbuf.at[rows(seq, TOK)], ks_sem, k_sem,
             device_id=(tm, peer), device_id_type=MESH,
@@ -99,7 +110,7 @@
         return carry
 
     def send_v(n, carry):
-        peer = seq_peer(n)
+        peer = seq_peer(NT - n)
         pltpu.make_async_remote_copy(
             v_ref.at[:, columns(peer)], vbuf.at[rows(seq, TOK)], vs_sem, v_sem,
             device_id=(tm, peer), device_id_type=MESH,
@@ -141,28 +152,33 @@
     take_all(kbuf, k_sem)
     take_all(vbuf, v_sem)
 
-    scale = HD ** (-0.5)
+    scale = HD ** (-0.5) * math.log2(math.e)
     nt = (((1,), (1,)), ((), ()))
 
     def attention(r):
         take_all(qbuf.at[r], q_sem.at[r])
         q = qbuf[r].reshape(4 * TOK, HD)
-        sv = lax.dot_general(q, kbuf[...], nt, preferred_element_type=F32) * scale
-        mv = jnp.max(sv, axis=-1, keepdims=True)
-        pv = jnp.exp(sv - mv)
-        lv = jnp.sum(pv, axis=-1, keepdims=True)
-        branch = []
-        for b in range(2):
-            st = lax.dot_general(q, text[b, 0], nt, preferred_element_type=F32) * scale
-            top = jnp.maximum(mv, jnp.max(st, axis=-1, keepdims=True))
-            pt = jnp.exp(st - top)
-            shift = jnp.exp(mv - top)
-            inverse = 1.0 / (lv * shift + jnp.sum(pt, axis=-1, keepdims=True))
-            wv = (pv * (shift * inverse)).astype(BF16)
-            wt = (pt * inverse).astype(BF16)
-            o = jnp.dot(wv, vbuf[...], preferred_element_type=F32)
-            o = o + jnp.dot(wt, text[b, 1], preferred_element_type=F32)
-            branch.append(o.astype(BF16).astype(F32))
+        halves = [q[: 2 * TOK], q[2 * TOK :]]
+        scores = [
+            [lax.dot_general(h, k, nt, preferred_element_type=F32) for k in (kbuf[...], text[0, 0], text[1, 0])]
+            for h in halves
+        ]
+        branch = [[], []]
+        for sv, *st in scores:
+            mv = jnp.max(sv, axis=-1, keepdims=True)
+            pv = jnp.exp2((sv - mv) * scale)
+            lv = jnp.sum(pv, axis=-1, keepdims=True)
+            for b in range(2):
+                top = jnp.maximum(mv, jnp.max(st[b], axis=-1, keepdims=True))
+                pt = jnp.exp2((st[b] - top) * scale)
+                shift = jnp.exp2((mv - top) * scale)
+                inverse = 1.0 / (lv * shift + jnp.sum(pt, axis=-1, keepdims=True))
+                wv = (pv * (shift * inverse)).astype(BF16)
+                wt = (pt * inverse).astype(BF16)
+                o = jnp.dot(wv, vbuf[...], preferred_element_type=F32)
+                o = o + jnp.dot(wt, text[b, 1], preferred_element_type=F32)
+                branch[b].append(o.astype(BF16).astype(F32))
+        branch = [jnp.concatenate(halves, axis=0) for halves in branch]
         cond, uncond = branch
         mixed = uncond + strength * (cond - uncond)
         ys = (y + 8 - y_offset(r)) % 8
@@ -170,7 +186,7 @@
             token_block = ((j // 2) * 16 + ys * 2 + j % 2) * 2
             for h in range(2):
                 part = slice((2 * j + h) * BLOCK, (2 * j + h + 1) * BLOCK)
-                guided_here = jnp.full((BLOCK, HD), mask_ref[token_block + h], jnp.int32) > 0
+                guided_here = jnp.full((BLOCK, HD), mask[token_block + h], jnp.int32) > 0
                 gbuf[r, j, h * BLOCK : (h + 1) * BLOCK] = jnp.where(
                     guided_here, mixed[part], cond[part]
                 ).astype(BF16)
@@ -225,50 +241,84 @@
         for k in range(NZ):
             drift = coef[k, 0:1] * (tjbuf[r, k].astype(F32) - pbuf[r, k].astype(F32))
             total = total + drift
-            obuf[r, k] = total
+            if k % 2 == 0:
+                sums[r, k // 2] = total
+        last[r] = total
 
         @pl.when(xh == 0)
         def _():
             pltpu.make_async_remote_copy(
-                obuf.at[r, NZ - 1], totbuf.at[r], tots_sem, tot_sem.at[r],
+                last.at[r], totbuf.at[r], tots_sem, tot_sem.at[r],
                 device_id=(NZ + z, seq), device_id_type=MESH,
             ).start()
 
-        window = (rows(role_h, HALF), columns(head_of(role_a, r)))
-        pltpu.make_async_copy(obuf.at[r, z], out_ref.at[window], o_sem).start()
-
-        def send(n, carry):
-            other = (z + n) % NZ
+        def send(other):
             pltpu.make_async_remote_copy(
-                obuf.at[r, other], out_ref.at[window], os_sem, o_sem,
+                sums.at[r, other // 2], fin.at[r, z], fs_sem, f_sem.at[r],
                 device_id=(xh * NZ + other, seq), device_id_type=MESH,
             ).start()
+
+        @pl.when(role_h == 0)
+        def _():
+            send((z + 5) % NZ)
+            send((z + 2) % NZ)
+            send((z + 7) % NZ)
+            send(z + 1)
+
+        @pl.when(role_h == 1)
+        def _():
+            send((z + 3) % NZ)
+            send((z + 6) % NZ)
+            send((z + 1) % NZ)
+            send(z - 1)
+
+        fin[r, z] = sums[r, role_a]
+
+    def relay(r):
+        take_all(fin.at[r, 0:4], f_sem.at[r])
+
+        def send(n, carry):
+            role = (z + NZ + (2 * role_h - 1) * n) % NZ
+            pltpu.make_async_remote_copy(
+                fin.at[r, role], fin.at[r, role], ls_sem, l_sem.at[r],
+                device_id=(xh * NZ + partner, seq), device_id_type=MESH,
+            ).start()
             return carry
 
-        lax.fori_loop(1, NZ, send, 0)
+        lax.fori_loop(1, 4, send, 0)
+
+    def finish(r):
+        take_all(fin.at[r, 0:3], l_sem.at[r])
+        for a in range(4):
+            head = head_of(a, r)
+            state = fin[r, 2 * a : 2 * a + 2].reshape(TOK, HD)
+            latent = own[:, columns(head)].astype(F32)
+            drift = coef[z, 0:1] * (latent - rbuf[r, a].astype(F32))
+            odd = jnp.full((TOK, HD), role_h, jnp.int32) > 0
+            obuf[r, a] = jnp.where(odd, state + drift, state)
+            pltpu.make_async_copy(obuf.at[r, a], out_ref.at[:, columns(head)], o_sem).start()
+
+    stages = (attention, to_steps, running_sum, relay, finish)
 
     def turn(t, carry):
-        @pl.when(t < ROUNDS)
-        def _():
-            attention(t)
-
-        @pl.when((t >= LAG1) & (t < ROUNDS + LAG1))
-        def _():
-            to_steps(t - LAG1)
-
-        @pl.when(t == LAG2)
+        @pl.when(t == 2)
         def _():
             take_all(stbuf, st_sem)
             take_all(tjbuf, tj_sem)
             take_all(coef.at[0 : NZ - 1], c_sem)
-
-        @pl.when(t >= LAG2)
-        def _():
-            running_sum(t - LAG2)
-
-        return carry
-
-    lax.fori_loop(0, ROUNDS + LAG2, turn, 0)
+            take_all(own, own_sem)
+
+        for lag, stage in zip(LAGS, stages):
+            if lag >= LAGS[2]:
+                lag = lag + xh * BEHIND
+
+            @pl.when((t >= lag) & (t < ROUNDS + lag))
+            def _(lag=lag, stage=stage):
+                stage(t - lag)
+
+        return carry
+
+    lax.fori_loop(0, ROUNDS + LAGS[-1] + BEHIND, turn, 0)
 
     take_all(kbuf.at[0 : (NT - 1) * TOK], ks_sem)
     take_all(vbuf.at[0 : (NT - 1) * TOK], vs_sem)
@@ -276,7 +326,8 @@
     take_all(kbuf.at[0 : (NT - 1) * TOK], rs_sem)
     take_all(tjbuf.at[:, 0 : NZ - 1], tjs_sem)
     take_all(pbuf.at[:, 0 : NZ - 1], ps_sem)
-    take_all(obuf.at[:, 0 : NZ - 1], os_sem)
+    take_all(sums, fs_sem)
+    take_all(fin.at[:, 0:3], ls_sem)
     take_all(coef.at[0 : NZ - 1], cs_sem)
 
     @pl.when(xh == 0)
@@ -288,18 +339,20 @@
 
 def per_device(queries, keys, values, text_kv, trajectory, start_latent, region_mask, timesteps):
     any_space = pl.BlockSpec(memory_space=pl.ANY)
-    smem = pl.BlockSpec(memory_space=pltpu.SMEM)
     dma, dma8 = pltpu.SemaphoreType.DMA, pltpu.SemaphoreType.DMA((ROUNDS,))
     out = pl.pallas_call(
         kernel,
         out_shape=jax.ShapeDtypeStruct(queries.shape[1:], F32),
-        in_specs=[smem, smem] + [any_space] * 6,
+        in_specs=[any_space] * 8,
         out_specs=any_space,
         scratch_shapes=[
+            pltpu.SMEM(region_mask.shape, jnp.int32),
+            pltpu.SMEM(timesteps.shape, jnp.int32),
             pltpu.VMEM((NT * TOK, HD), BF16),
             pltpu.VMEM((NT * TOK, HD), BF16),
             pltpu.VMEM((ROUNDS, 4, TOK, HD), BF16),
             pltpu.VMEM(text_kv.shape, BF16),
+            pltpu.VMEM(trajectory.shape[1:], BF16),
             pltpu.VMEM((ROUNDS, 4, TOK, HD), BF16),
             pltpu.VMEM((ROUNDS, 4, TOK, HD), BF16),
             pltpu.VMEM((ROUNDS, NZ, HALF, HD), BF16),
@@ -307,13 +360,18 @@
             pltpu.VMEM((ROUNDS, HALF, HD), BF16),
             pltpu.VMEM((ROUNDS, HALF, HD), F32),
             pltpu.VMEM((HALF, HD), F32),
+            pltpu.VMEM((ROUNDS, NZ // 2, HALF, HD), F32),
+            pltpu.VMEM((ROUNDS, HALF, HD), F32),
             pltpu.VMEM((ROUNDS, NZ, HALF, HD), F32),
+            pltpu.VMEM((ROUNDS, 4, TOK, HD), F32),
             pltpu.VMEM((NZ, 8, HD), F32),
-            dma, dma, dma8, dma8, dma8, dma, dma, dma8, dma, dma, dma,
-            dma, dma, dma, dma, dma, dma, dma, dma, dma,
+            pltpu.SemaphoreType.DMA((2,)),
+            dma, dma, dma8, dma8, dma8, dma, dma, dma8, dma8, dma8, dma,
+            dma, dma, dma,
+            dma, dma, dma, dma, dma, dma, dma, dma, dma, dma,
         ],
         compiler_params=pltpu.CompilerParams(
-            collective_id=0, has_side_effects=True, vmem_limit_bytes=48 << 20
+            collective_id=0, has_side_effects=True, vmem_limit_bytes=62 << 20
         ),
     )(
         region_mask, timesteps, queries[0], keys[0], values[0], text_kv, trajectory[0], start_latent

time: 104 us -> 90.7 us (0.87)
  Pallas kernels: 95.5 us -> 88 us
  local copies, waits for them, and re-layouts: 7.89 us -> 2.27 us
    pallas_call x1, Pallas kernels: 95.5 us -> 88 us  [per_device(): pl.pallas_call(kernel, out_shape=jax.ShapeDtypeStruct(queries.shape[1:],...]
    unnamed x17 -> x1, local copies, waits for them, and re-layouts: 7.89 us -> 2.27 us
where the time goes in v2:
time: 90.7 us; the launch traced here: 90.3 us
  Pallas kernels  88 us (97%)
  local copies, waits for them, and re-layouts  2.27 us (3%)
    pallas_call x1, Pallas kernels, per_device(): pl.pallas_call(kernel, out_shape=jax.ShapeDtypeStruct(queries.shape[1:],...  88 us
    unnamed x1, local copies, waits for them, and re-layouts  2.27 us

profile of v2, /device:TPU:6, one launch (start us, length us, event | category | flops | bytes accessed | tf_op | source)
XLA Modules:
  0.0 90.3 jit_solution(13540276066991595445)
XLA Ops:
  0.0 88.0 %shard_map.82 = f32[64,4096]{1,0:T(8,128)} custom-call(s32[64]{0:T(128)} %mask_ref.1, s32[1,2]{1,0:T(1,128)} %ts_ref.1, bf16[64,4096]{1,0:T(8,128)(2,1)} %bitcast.6, bf16[64,4096]{1,0:T(8,128)(2,1)} %bitcast.7, bf16[64,4096]{1,0:T(8,128)(2,1)} %bitcast.8, bf16[2,2,512,128]{3,2,1,0:T(8,128)(2,1)} %text_ref.1, bf16[64,4096]{1,0:T(8,128)(2,1)} %bitcast.9, ...), custom_call_target="tpu_custom_call" | custom-call | tf_op jit(solution)/shard_map/pallas_call | solution.py:343
  88.0 2.3 %copy.10 = f32[1,64,4096]{2,1,0:T(8,128)} copy(f32[1,64,4096]{2,1,0:T(8,128)} %bitcast.5) | data formatting | bytes 2097152

commit v3 on v2

--- a/solution.py
+++ b/solution.py
@@ -14,8 +14,9 @@
 NT = 32
 NZ = 8
 ROUNDS = 8
-LAGS = (0, 2, 4, 6, 8)
-BEHIND = 2
+LAGS = (0, 3, 5, 7, 9)
+DIRECT = 6
+BEHIND = 1
 MESH = pl.DeviceIdType.MESH
 F32 = jnp.float32
 BF16 = jnp.bfloat16
@@ -36,7 +37,7 @@
     fin, obuf, coef,
     small_sem, k_sem, v_sem, q_sem, r_sem, p_sem, tj_sem, st_sem, tot_sem, f_sem, l_sem, o_sem,
     c_sem, text_sem, own_sem,
-    ks_sem, vs_sem, qs_sem, rs_sem, ps_sem, tjs_sem, tots_sem, fs_sem, ls_sem, cs_sem,
+    ks_sem, vs_sem, qs_sem, rs_sem, ps_sem, tjs_sem, tots_sem, fs_sem, ds_sem, ls_sem, cs_sem,
 ):
     tm, seq = lax.axis_index("tm"), lax.axis_index("seq")
     xh, z = tm // NZ, tm % NZ
@@ -252,43 +253,60 @@
                 device_id=(NZ + z, seq), device_id_type=MESH,
             ).start()
 
-        def send(other):
+        def send(other, sent=fs_sem):
             pltpu.make_async_remote_copy(
-                sums.at[r, other // 2], fin.at[r, z], fs_sem, f_sem.at[r],
+                sums.at[r, other // 2], fin.at[r, z], sent, f_sem.at[r],
                 device_id=(xh * NZ + other, seq), device_id_type=MESH,
             ).start()
 
-        @pl.when(role_h == 0)
+        @pl.when((r < DIRECT) & (role_h == 0))
         def _():
             send((z + 5) % NZ)
             send((z + 2) % NZ)
             send((z + 7) % NZ)
             send(z + 1)
 
-        @pl.when(role_h == 1)
+        @pl.when((r < DIRECT) & (role_h == 1))
         def _():
             send((z + 3) % NZ)
             send((z + 6) % NZ)
             send((z + 1) % NZ)
             send(z - 1)
 
+        @pl.when(r >= DIRECT)
+        def _():
+            def send_to(n, carry):
+                send((z + n) % NZ, ds_sem)
+                return carry
+
+            lax.fori_loop(1, NZ, send_to, 0)
+
         fin[r, z] = sums[r, role_a]
 
     def relay(r):
-        take_all(fin.at[r, 0:4], f_sem.at[r])
-
-        def send(n, carry):
-            role = (z + NZ + (2 * role_h - 1) * n) % NZ
-            pltpu.make_async_remote_copy(
-                fin.at[r, role], fin.at[r, role], ls_sem, l_sem.at[r],
-                device_id=(xh * NZ + partner, seq), device_id_type=MESH,
-            ).start()
-            return carry
-
-        lax.fori_loop(1, 4, send, 0)
+        @pl.when(r < DIRECT)
+        def _():
+            take_all(fin.at[r, 0:4], f_sem.at[r])
+
+            def send(n, carry):
+                role = (z + NZ + (2 * role_h - 1) * n) % NZ
+                pltpu.make_async_remote_copy(
+                    fin.at[r, role], fin.at[r, role], ls_sem, l_sem.at[r],
+                    device_id=(xh * NZ + partner, seq), device_id_type=MESH,
+                ).start()
+                return carry
+
+            lax.fori_loop(1, 4, send, 0)
 
     def finish(r):
-        take_all(fin.at[r, 0:3], l_sem.at[r])
+        @pl.when(r < DIRECT)
+        def _():
+            take_all(fin.at[r, 0:3], l_sem.at[r])
+
+        @pl.when(r >= DIRECT)
+        def _():
+            take_all(fin.at[r, 0 : NZ - 1], f_sem.at[r])
+
         for a in range(4):
             head = head_of(a, r)
             state = fin[r, 2 * a : 2 * a + 2].reshape(TOK, HD)
@@ -326,8 +344,9 @@
     take_all(kbuf.at[0 : (NT - 1) * TOK], rs_sem)
     take_all(tjbuf.at[:, 0 : NZ - 1], tjs_sem)
     take_all(pbuf.at[:, 0 : NZ - 1], ps_sem)
-    take_all(sums, fs_sem)
-    take_all(fin.at[:, 0:3], ls_sem)
+    take_all(sums.at[0:DIRECT], fs_sem)
+    take_all(fin.at[0 : ROUNDS - DIRECT, 0 : NZ - 1], ds_sem)
+    take_all(fin.at[0:DIRECT, 0:3], ls_sem)
     take_all(coef.at[0 : NZ - 1], cs_sem)
 
     @pl.when(xh == 0)
@@ -368,7 +387,7 @@
             pltpu.SemaphoreType.DMA((2,)),
             dma, dma, dma8, dma8, dma8, dma, dma, dma8, dma8, dma8, dma,
             dma, dma, dma,
-            dma, dma, dma, dma, dma, dma, dma, dma, dma, dma,
+            dma, dma, dma, dma, dma, dma, dma, dma, dma, dma, dma,
         ],
         compiler_params=pltpu.CompilerParams(
             collective_id=0, has_side_effects=True, vmem_limit_bytes=62 << 20

time: 90.7 us -> 89.2 us (0.983)
  Pallas kernels: 88 us -> 86.7 us
    pallas_call x1, Pallas kernels: 88 us -> 86.7 us  [per_device(): pl.pallas_call(kernel, out_shape=jax.ShapeDtypeStruct(queries.shape[1:],...]
where the time goes in v3:
time: 89.2 us; the launch traced here: 89 us
  Pallas kernels  86.7 us (97%)
  local copies, waits for them, and re-layouts  2.27 us (3%)
    pallas_call x1, Pallas kernels, per_device(): pl.pallas_call(kernel, out_shape=jax.ShapeDtypeStruct(queries.shape[1:],...  86.7 us
    unnamed x1, local copies, waits for them, and re-layouts  2.27 us

profile of v3, /device:TPU:6, one launch (start us, length us, event | category | flops | bytes accessed | tf_op | source)
XLA Modules:
  0.0 89.0 jit_solution(13109867225847206766)
XLA Ops:
  0.0 86.7 %shard_map.82 = f32[64,4096]{1,0:T(8,128)} custom-call(s32[64]{0:T(128)} %mask_ref.1, s32[1,2]{1,0:T(1,128)} %ts_ref.1, bf16[64,4096]{1,0:T(8,128)(2,1)} %bitcast.6, bf16[64,4096]{1,0:T(8,128)(2,1)} %bitcast.7, bf16[64,4096]{1,0:T(8,128)(2,1)} %bitcast.8, bf16[2,2,512,128]{3,2,1,0:T(8,128)(2,1)} %text_ref.1, bf16[64,4096]{1,0:T(8,128)(2,1)} %bitcast.9, ...), custom_call_target="tpu_custom_call" | custom-call | tf_op jit(solution)/shard_map/pallas_call | solution.py:362
  86.7 2.3 %copy.10 = f32[1,64,4096]{2,1,0:T(8,128)} copy(f32[1,64,4096]{2,1,0:T(8,128)} %bitcast.5) | data formatting | bytes 2097152
